TPU v7x, 512 devices: a whole 4x4x16 slice. The times are simulated.
512 devices in a mesh: recv: 128 (over z, x, core), src: 4 (over y).
Axes of the slice: x: 4, y: 4, z: 16, core: 2. Of those that a mesh axis runs over, the one named last changes fastest.
Arguments:
- interactions: int32 [3, 49152], P(None, ('recv', 'src')), may hold values from 0 to 4095, as said below
- list_lengths: int32 [512], P(('recv', 'src')), may hold values from 48 to 96, as said below
- kernels: float32 [2048, 128, 16, 128], P(('recv', 'src')), may hold values from -0.0210316469 to 0.0210316469
- prestress: float32 [4096, 128], P(('recv', 'src')), may hold values from 2 to 3
- friction: float32 [4096, 128], P(('recv', 'src')), may hold values from 0.2 to 0.5
- load_rate: float32 [4096, 128], P(('recv', 'src')), may hold values from 0.04 to 0.08
Outputs:
- slip_rates: float32 [4096, 96, 128], P(('recv', 'src'))
Inputs may be any that keep to these rules, and one draw needn't show every extreme that they name: `interactions`: column e belongs to device block g = e // 96, g = i * 4 + j. Its receiver patch lies in [i * 4 * 8, (i + 1) * 4 * 8); its source patch p satisfies (p // 8) mod 4 == j; its owner is p // 32; its lag offset lies in [32, 48]. The entries of one block name at most 1 distinct source patches of one owner, and in every draw some owner supplies exactly that many distinct source patches to every block. `list_lengths`: some device's list is full and some device's list holds exactly half, in every draw.
All inputs are finite; a program needn't handle non-finite values.
Results may differ from a plain program's by a relative error of at most 0.0003.
Values sent between devices are 32-bit elements; how exact they have to be, the bound alone decides.
A program may use at most 128 MiB of HBM per device.

v0:
```python
import jax
import jax.numpy as jnp
from jax import lax
from jax.sharding import PartitionSpec as P

BLOCK = 32
BLOCKS = 3
NEWTON = 4
damping = 0.5


def inverse_sinh(values):
    magnitude = jnp.abs(values)
    result = jnp.log(magnitude + jnp.sqrt(1.0 + magnitude * magnitude))
    return jnp.where(values < 0, -result, result)


def friction_solve(drive, friction):
    rates = jnp.zeros_like(drive)
    for newton_step in range(NEWTON):
        misfit = damping * rates + friction * inverse_sinh(rates) - drive
        slope_now = damping + friction * lax.rsqrt(1.0 + rates * rates)
        rates = rates - misfit / slope_now
    return rates


def local(interactions, list_lengths, kernels, prestress, friction, load_rate):
    n_recv = lax.axis_size("recv")
    n_src = lax.axis_size("src")
    recv_idx = lax.axis_index("recv")
    src_idx = lax.axis_index("src")
    ent_count = interactions.shape[1]
    ker_count = kernels.shape[0]
    width = kernels.shape[1]
    lag_count = kernels.shape[2]
    patch_count = prestress.shape[0]
    per_kernel = ent_count // ker_count
    peer_cap = max(1, ent_count // (8 * n_recv))
    group_rows = n_src * patch_count
    receivers = interactions[0] - recv_idx * group_rows
    sources = interactions[1]
    owners = sources // group_rows
    local_patch = sources % patch_count
    delays = interactions[2]
    entry_numbers = jnp.arange(ent_count, dtype=jnp.int32)
    same_source = sources[None, :] == sources[:, None]
    first_of = jnp.min(jnp.where(same_source, entry_numbers[None, :], ent_count), axis=1)
    is_first = first_of == entry_numbers
    earlier = (
        (owners[None, :] == owners[:, None])
        & is_first[None, :]
        & (entry_numbers[None, :] < first_of[:, None])
    )
    ranks = jnp.sum(earlier.astype(jnp.int32), axis=1)
    slot_of = owners * peer_cap + ranks
    slot_ids = jnp.arange(n_recv * peer_cap, dtype=jnp.int32)
    filling = (slot_ids[:, None] == slot_of[None, :]) & is_first[None, :]
    wanted = jnp.sum(jnp.where(filling, local_patch[None, :], 0), axis=1)
    asked = lax.all_to_all(
        wanted.reshape(n_recv, peer_cap), "recv", split_axis=0, concat_axis=0, tiled=True
    ).reshape(-1)
    live = (entry_numbers < list_lengths[0]).astype(jnp.float32)
    patch_ids = jnp.arange(group_rows, dtype=jnp.int32)
    route_table = jnp.where(patch_ids[:, None] == receivers[None, :], live[None, :], 0.0)
    kernel_matrices = kernels.reshape(ker_count, width, lag_count * width)

    def cut_window(window, delay):
        return lax.dynamic_slice_in_dim(
            window, 2 * BLOCK - delay - (lag_count - 1), BLOCK + lag_count - 1, 0
        )

    def one_kernel(pair):
        segs, kern = pair
        pieces = [
            segs[:, lag_count - 1 - lag_idx : lag_count - 1 - lag_idx + BLOCK]
            for lag_idx in range(lag_count)
        ]
        stacked_rows = jnp.stack(pieces, axis=2).reshape(per_kernel * BLOCK, lag_count * width)
        return jnp.einsum("mk,rk->mr", stacked_rows, kern, precision=lax.Precision.HIGHEST)

    finished_blocks = []
    for block_idx in range(BLOCKS):
        if block_idx == 0:
            stress = jnp.zeros((patch_count, BLOCK, width), jnp.float32)
        else:
            recent = jnp.concatenate(finished_blocks[max(0, block_idx - 2) :], axis=1)
            span = recent.shape[1]
            outgoing = jnp.take(recent, asked, axis=0).reshape(n_recv, peer_cap, span, width)
            received = lax.all_to_all(outgoing, "recv", split_axis=0, concat_axis=0, tiled=True)
            picked = jnp.take(received.reshape(n_recv * peer_cap, span, width), slot_of, axis=0)
            windows = jnp.pad(picked, ((0, 0), (2 * BLOCK - span, 0), (0, 0)))
            segments = jax.vmap(cut_window)(windows, delays)
            grouped = segments.reshape(ker_count, per_kernel, BLOCK + lag_count - 1, width)
            stress_terms = lax.map(one_kernel, (grouped, kernel_matrices)).reshape(
                ent_count, BLOCK * width
            )
            summed = jnp.dot(route_table, stress_terms, precision=lax.Precision.HIGHEST)
            partial_terms = summed.reshape(group_rows, BLOCK, width)
            summed_all = lax.psum(partial_terms, "src")
            stress = lax.dynamic_slice_in_dim(summed_all, src_idx * patch_count, patch_count, 0)
        times = (block_idx * BLOCK + 1 + jnp.arange(BLOCK, dtype=jnp.int32)).astype(jnp.float32)
        drive = prestress[:, None, :] + load_rate[:, None, :] * times[None, :, None] + stress
        finished_blocks.append(friction_solve(drive, friction[:, None, :]))
    return jnp.concatenate(finished_blocks, axis=1)


def solution(mesh):
    in_specs = (
        P(None, ("recv", "src")),
        P(("recv", "src")),
        P(("recv", "src"), None, None, None),
        P(("recv", "src"), None),
        P(("recv", "src"), None),
        P(("recv", "src"), None),
    )
    out_specs = P(("recv", "src"), None, None)
    return jax.shard_map(local, mesh=mesh, in_specs=in_specs, out_specs=out_specs, check_vma=False)
```

profile of v0, /device:TPU:2, one launch (start us, length us, event | category | flops | bytes accessed | tf_op | source)
XLA Modules:
  0.0 748.2 jit_solution(15495887555175844307)
XLA Ops:
  9.3 19.4 %all-to-all-start = ((s32[128,1,1]{2,1,0:T(1,128)}), s32[128,1,1]{2,1,0:T(1,128)S(1)}, u32[]{:S(2)}, u32[]{:S(2)}) async-start(s32[128,1,1]{2,1,0:T(1,128)} %copy.163), calls=%async_computation | async-start | bytes 131072 | tf_op jit(solution)/shard_map/all_to_all | solution.py:59
  30.6 11.9 %all-to-all-done = s32[128,1,1]{2,1,0:T(1,128)S(1)} async-done(((s32[128,1,1]{2,1,0:T(1,128)}), s32[128,1,1]{2,1,0:T(1,128)S(1)}, u32[]{:S(2)}, u32[]{:S(2)}) %all-to-all-start) | async-done | bytes 544 | tf_op jit(solution)/shard_map/all_to_all | solution.py:59
  42.5 2.3 reduce
  47.3 6.7 all-to-all-start.1
  54.4 5.0 reshape.247
  60.6 89.8 %all-to-all-done.1 = f32[128,1,32,128]{3,2,1,0:T(8,128)S(1)} async-done(((f32[128,1,32,128]{3,2,1,0:T(8,128)}), f32[128,1,32,128]{3,2,1,0:T(8,128)S(1)}, u32[]{:S(2)}, u32[]{:S(2)}) %all-to-all-start.1) | async-done | bytes 2097184 | tf_op jit(solution)/shard_map/all_to_all | solution.py:89
  155.2 8.5 %gather_fusion.4 = f32[96,47,128]{2,0,1:T(8,128)} fusion(f32[96,64,128]{2,0,1:T(8,128)S(1)} %pad.5.clone, s32[96]{0:T(128)S(1)} %get-tuple-element.145), kind=kCustom, calls=%fused_computation.4 | custom fusion | bytes 4621440 | tf_op jit(solution)/shard_map/vmap()/gather | solution.py:68
  165.0 117.7 %while.20 = (s32[]{:T(128)}, f32[4,768,128]{2,1,0:T(8,128)}, f32[4,24,47,128]{3,1,0,2:T(8,128)}, f32[4,128,2048]{2,1,0:T(8,128)}, s32[]{:T(128)}) while((s32[]{:T(128)}, f32[4,768,128]{2,1,0:T(8,128)}, f32[4,24,47,128]{3,1,0,2:T(8,128)}, f32[4,128,2048]{2,1,0:T(8,128)}, s32[]{:T(128)}) %tuple.92), condition=%wide.region_4.5_spmd, body=%wide.region_3.4_spmd.sunk | while | flops 2415919104 | bytes 35210304 | solution.py:94
  168.7 16.2 %stack.104 = f32[24,32,16,128]{3,2,1,0:T(8,128)} concatenate(f32[24,32,1,128]{3,2,1,0:T(1,128)} %bitcast.321, f32[24,32,1,128]{3,2,1,0:T(1,128)} %bitcast.320, f32[24,32,1,128]{3,2,1,0:T(1,128)} %bitcast.319, f32[24,32,1,128]{3,2,1,0:T(1,128)} %bitcast.318, f32[24,32,1,128]{3,2,1,0:T(1,128)} %bitcast.317, f32[24,32,1,128]{3,2,1,0:T(1,128)} %bitcast.316, ...), dimensions={2} | concatenate | bytes 12582912 | tf_op jit(solution)/shard_map/while/body/eval_jaxpr/stack | solution.py:78
  184.9 9.9 %fusion.111 = f32[4,768,128]{2,1,0:T(8,128)} fusion(f32[4,768,128]{2,1,0:T(8,128)} %get-tuple-element.267, s32[]{:T(128)} %get-tuple-element.266, f32[96,8,16,128]{3,2,1,0:T(8,128)} %bitcast.304, f32[4,128,2048]{2,1,0:T(8,128)} %get-tuple-element.274), kind=kOutput, calls=%fused_computation.10.clone.1 | convolution fusion | flops 2415919104 | bytes 7734272 | tf_op jit(solution)/shard_map/while/body/eval_jaxpr/mk,rk->mr/dot_general | solution.py:79
  198.0 16.2 %stack.104 = f32[24,32,16,128]{3,2,1,0:T(8,128)} concatenate(f32[24,32,1,128]{3,2,1,0:T(1,128)} %bitcast.321, f32[24,32,1,128]{3,2,1,0:T(1,128)} %bitcast.320, f32[24,32,1,128]{3,2,1,0:T(1,128)} %bitcast.319, f32[24,32,1,128]{3,2,1,0:T(1,128)} %bitcast.318, f32[24,32,1,128]{3,2,1,0:T(1,128)} %bitcast.317, f32[24,32,1,128]{3,2,1,0:T(1,128)} %bitcast.316, ...), dimensions={2} | concatenate | bytes 12582912 | tf_op jit(solution)/shard_map/while/body/eval_jaxpr/stack | solution.py:78
  214.2 9.9 %fusion.111 = f32[4,768,128]{2,1,0:T(8,128)} fusion(f32[4,768,128]{2,1,0:T(8,128)} %get-tuple-element.267, s32[]{:T(128)} %get-tuple-element.266, f32[96,8,16,128]{3,2,1,0:T(8,128)} %bitcast.304, f32[4,128,2048]{2,1,0:T(8,128)} %get-tuple-element.274), kind=kOutput, calls=%fused_computation.10.clone.1 | convolution fusion | flops 2415919104 | bytes 7734272 | tf_op jit(solution)/shard_map/while/body/eval_jaxpr/mk,rk->mr/dot_general | solution.py:79
  227.3 16.2 %stack.104 = f32[24,32,16,128]{3,2,1,0:T(8,128)} concatenate(f32[24,32,1,128]{3,2,1,0:T(1,128)} %bitcast.321, f32[24,32,1,128]{3,2,1,0:T(1,128)} %bitcast.320, f32[24,32,1,128]{3,2,1,0:T(1,128)} %bitcast.319, f32[24,32,1,128]{3,2,1,0:T(1,128)} %bitcast.318, f32[24,32,1,128]{3,2,1,0:T(1,128)} %bitcast.317, f32[24,32,1,128]{3,2,1,0:T(1,128)} %bitcast.316, ...), dimensions={2} | concatenate | bytes 12582912 | tf_op jit(solution)/shard_map/while/body/eval_jaxpr/stack | solution.py:78
  243.5 9.9 %fusion.111 = f32[4,768,128]{2,1,0:T(8,128)} fusion(f32[4,768,128]{2,1,0:T(8,128)} %get-tuple-element.267, s32[]{:T(128)} %get-tuple-element.266, f32[96,8,16,128]{3,2,1,0:T(8,128)} %bitcast.304, f32[4,128,2048]{2,1,0:T(8,128)} %get-tuple-element.274), kind=kOutput, calls=%fused_computation.10.clone.1 | convolution fusion | flops 2415919104 | bytes 7734272 | tf_op jit(solution)/shard_map/while/body/eval_jaxpr/mk,rk->mr/dot_general | solution.py:79
  256.5 16.2 %stack.104 = f32[24,32,16,128]{3,2,1,0:T(8,128)} concatenate(f32[24,32,1,128]{3,2,1,0:T(1,128)} %bitcast.321, f32[24,32,1,128]{3,2,1,0:T(1,128)} %bitcast.320, f32[24,32,1,128]{3,2,1,0:T(1,128)} %bitcast.319, f32[24,32,1,128]{3,2,1,0:T(1,128)} %bitcast.318, f32[24,32,1,128]{3,2,1,0:T(1,128)} %bitcast.317, f32[24,32,1,128]{3,2,1,0:T(1,128)} %bitcast.316, ...), dimensions={2} | concatenate | bytes 12582912 | tf_op jit(solution)/shard_map/while/body/eval_jaxpr/stack | solution.py:78
  272.8 9.9 %fusion.111 = f32[4,768,128]{2,1,0:T(8,128)} fusion(f32[4,768,128]{2,1,0:T(8,128)} %get-tuple-element.267, s32[]{:T(128)} %get-tuple-element.266, f32[96,8,16,128]{3,2,1,0:T(8,128)} %bitcast.304, f32[4,128,2048]{2,1,0:T(8,128)} %get-tuple-element.274), kind=kOutput, calls=%fused_computation.10.clone.1 | convolution fusion | flops 2415919104 | bytes 7734272 | tf_op jit(solution)/shard_map/while/body/eval_jaxpr/mk,rk->mr/dot_general | solution.py:79
  286.1 54.1 %all-reduce.5.cloned.1.call-done = f32[32,32,128]{2,0,1:T(8,128)} async-done(((f32[32,32,128]{2,0,1:T(8,128)}), f32[32,32,128]{2,0,1:T(8,128)}) %all-reduce.5.cloned.1.call-update) | async-done | bytes 524304 | tf_op jit(solution)/shard_map/psum | solution.py:99
  341.7 2.8 gather_fusion.2
  344.4 2.5 fusion.24
  347.0 201.0 %all_to_all.25 = f32[128,1,64,128]{3,2,1,0:T(8,128)} all-to-all(f32[128,1,64,128]{3,2,1,0:T(8,128)S(1)} %fusion.24), channel_id=1, replica_groups=mesh['recv'=128,'src'=4] {'recv'}, dimensions={0} | all-to-all | bytes 8388608 | tf_op jit(solution)/shard_map/all_to_all | solution.py:89
  548.0 2.9 gather_fusion.3
  553.1 8.5 %gather_fusion.5 = f32[96,47,128]{2,0,1:T(8,128)} fusion(f32[96,64,128]{2,0,1:T(8,128)S(1)} %copy.171, s32[96]{0:T(128)S(1)} %get-tuple-element.145), kind=kCustom, calls=%fused_computation.5 | custom fusion | bytes 4621440 | tf_op jit(solution)/shard_map/vmap()/gather | solution.py:68
  562.8 117.4 %while.21 = (s32[]{:T(128)}, f32[4,768,128]{2,1,0:T(8,128)}, f32[4,24,47,128]{3,1,0,2:T(8,128)}, f32[4,128,2048]{2,1,0:T(8,128)}, s32[]{:T(128)}) while((s32[]{:T(128)}, f32[4,768,128]{2,1,0:T(8,128)}, f32[4,24,47,128]{3,1,0,2:T(8,128)}, f32[4,128,2048]{2,1,0:T(8,128)}, s32[]{:T(128)}) %tuple.91), condition=%wide.region_7.8_spmd, body=%wide.region_6.7_spmd.sunk | while | flops 2415919104 | bytes 35210304 | solution.py:94
  566.2 16.2 %stack.105 = f32[24,32,16,128]{3,2,1,0:T(8,128)} concatenate(f32[24,32,1,128]{3,2,1,0:T(1,128)} %bitcast.337, f32[24,32,1,128]{3,2,1,0:T(1,128)} %bitcast.336, f32[24,32,1,128]{3,2,1,0:T(1,128)} %bitcast.335, f32[24,32,1,128]{3,2,1,0:T(1,128)} %bitcast.334, f32[24,32,1,128]{3,2,1,0:T(1,128)} %bitcast.333, f32[24,32,1,128]{3,2,1,0:T(1,128)} %bitcast.332, ...), dimensions={2} | concatenate | bytes 12582912 | tf_op jit(solution)/shard_map/while/body/eval_jaxpr/stack | solution.py:78
  582.4 9.9 %fusion.115 = f32[4,768,128]{2,1,0:T(8,128)} fusion(f32[4,768,128]{2,1,0:T(8,128)} %get-tuple-element.282, s32[]{:T(128)} %get-tuple-element.281, f32[96,8,16,128]{3,2,1,0:T(8,128)} %bitcast.305, f32[4,128,2048]{2,1,0:T(8,128)} %get-tuple-element.289), kind=kOutput, calls=%fused_computation.20.clone.1 | convolution fusion | flops 2415919104 | bytes 7734272 | tf_op jit(solution)/shard_map/while/body/eval_jaxpr/mk,rk->mr/dot_general | solution.py:79
  595.5 16.2 %stack.105 = f32[24,32,16,128]{3,2,1,0:T(8,128)} concatenate(f32[24,32,1,128]{3,2,1,0:T(1,128)} %bitcast.337, f32[24,32,1,128]{3,2,1,0:T(1,128)} %bitcast.336, f32[24,32,1,128]{3,2,1,0:T(1,128)} %bitcast.335, f32[24,32,1,128]{3,2,1,0:T(1,128)} %bitcast.334, f32[24,32,1,128]{3,2,1,0:T(1,128)} %bitcast.333, f32[24,32,1,128]{3,2,1,0:T(1,128)} %bitcast.332, ...), dimensions={2} | concatenate | bytes 12582912 | tf_op jit(solution)/shard_map/while/body/eval_jaxpr/stack | solution.py:78
  611.7 9.9 %fusion.115 = f32[4,768,128]{2,1,0:T(8,128)} fusion(f32[4,768,128]{2,1,0:T(8,128)} %get-tuple-element.282, s32[]{:T(128)} %get-tuple-element.281, f32[96,8,16,128]{3,2,1,0:T(8,128)} %bitcast.305, f32[4,128,2048]{2,1,0:T(8,128)} %get-tuple-element.289), kind=kOutput, calls=%fused_computation.20.clone.1 | convolution fusion | flops 2415919104 | bytes 7734272 | tf_op jit(solution)/shard_map/while/body/eval_jaxpr/mk,rk->mr/dot_general | solution.py:79
  624.8 16.2 %stack.105 = f32[24,32,16,128]{3,2,1,0:T(8,128)} concatenate(f32[24,32,1,128]{3,2,1,0:T(1,128)} %bitcast.337, f32[24,32,1,128]{3,2,1,0:T(1,128)} %bitcast.336, f32[24,32,1,128]{3,2,1,0:T(1,128)} %bitcast.335, f32[24,32,1,128]{3,2,1,0:T(1,128)} %bitcast.334, f32[24,32,1,128]{3,2,1,0:T(1,128)} %bitcast.333, f32[24,32,1,128]{3,2,1,0:T(1,128)} %bitcast.332, ...), dimensions={2} | concatenate | bytes 12582912 | tf_op jit(solution)/shard_map/while/body/eval_jaxpr/stack | solution.py:78
  641.0 9.9 %fusion.115 = f32[4,768,128]{2,1,0:T(8,128)} fusion(f32[4,768,128]{2,1,0:T(8,128)} %get-tuple-element.282, s32[]{:T(128)} %get-tuple-element.281, f32[96,8,16,128]{3,2,1,0:T(8,128)} %bitcast.305, f32[4,128,2048]{2,1,0:T(8,128)} %get-tuple-element.289), kind=kOutput, calls=%fused_computation.20.clone.1 | convolution fusion | flops 2415919104 | bytes 7734272 | tf_op jit(solution)/shard_map/while/body/eval_jaxpr/mk,rk->mr/dot_general | solution.py:79
  654.1 16.2 %stack.105 = f32[24,32,16,128]{3,2,1,0:T(8,128)} concatenate(f32[24,32,1,128]{3,2,1,0:T(1,128)} %bitcast.337, f32[24,32,1,128]{3,2,1,0:T(1,128)} %bitcast.336, f32[24,32,1,128]{3,2,1,0:T(1,128)} %bitcast.335, f32[24,32,1,128]{3,2,1,0:T(1,128)} %bitcast.334, f32[24,32,1,128]{3,2,1,0:T(1,128)} %bitcast.333, f32[24,32,1,128]{3,2,1,0:T(1,128)} %bitcast.332, ...), dimensions={2} | concatenate | bytes 12582912 | tf_op jit(solution)/shard_map/while/body/eval_jaxpr/stack | solution.py:78
  670.3 9.9 %fusion.115 = f32[4,768,128]{2,1,0:T(8,128)} fusion(f32[4,768,128]{2,1,0:T(8,128)} %get-tuple-element.282, s32[]{:T(128)} %get-tuple-element.281, f32[96,8,16,128]{3,2,1,0:T(8,128)} %bitcast.305, f32[4,128,2048]{2,1,0:T(8,128)} %get-tuple-element.289), kind=kOutput, calls=%fused_computation.20.clone.1 | convolution fusion | flops 2415919104 | bytes 7734272 | tf_op jit(solution)/shard_map/while/body/eval_jaxpr/mk,rk->mr/dot_general | solution.py:79
  683.5 55.3 %all-reduce.7.cloned.1.call-done = f32[32,32,128]{2,0,1:T(8,128)} async-done(((f32[32,32,128]{2,0,1:T(8,128)}), f32[32,32,128]{2,0,1:T(8,128)}) %all-reduce.7.cloned.1.call-update) | async-done | bytes 524304 | tf_op jit(solution)/shard_map/psum | solution.py:99
  (117 shorter events, 52.7 us)
Async XLA Ops:
  9.3 33.3 %all-to-all-start = ((s32[128,1,1]{2,1,0:T(1,128)}), s32[128,1,1]{2,1,0:T(1,128)S(1)}, u32[]{:S(2)}, u32[]{:S(2)}) async-start(s32[128,1,1]{2,1,0:T(1,128)} %copy.163), calls=%async_computation | async-start | bytes 131072 | tf_op jit(solution)/shard_map/all_to_all | solution.py:59
  29.4 15.5 %copy-start.7 = (f32[8,128]{1,0:T(8,128)}, f32[8,128]{1,0:T(8,128)S(1)}, u32[]{:S(2)}) copy-start(f32[8,128]{1,0:T(8,128)S(1)} %get-tuple-element.139) | copy-start | bytes 12292
  29.4 15.5 %copy-start.10 = (f32[8,128]{1,0:T(8,128)}, f32[8,128]{1,0:T(8,128)S(1)}, u32[]{:S(2)}) copy-start(f32[8,128]{1,0:T(8,128)S(1)} %get-tuple-element.140) | copy-start | bytes 12292
  30.6 14.4 %copy-start = (f32[8,32,128]{2,0,1:T(8,128)}, f32[8,32,128]{2,0,1:T(8,128)S(1)}, u32[]{:S(2)}) copy-start(f32[8,32,128]{2,0,1:T(8,128)S(1)} %fusion.46) | copy-start | bytes 393220
  44.9 2.4 copy-start.13
  47.3 103.2 %all-to-all-start.1 = ((f32[128,1,32,128]{3,2,1,0:T(8,128)}), f32[128,1,32,128]{3,2,1,0:T(8,128)S(1)}, u32[]{:S(2)}, u32[]{:S(2)}) async-start(f32[128,1,32,128]{3,2,1,0:T(8,128)} %fusion.25), calls=%async_computation.1 | async-start | bytes 4194304 | tf_op jit(solution)/shard_map/all_to_all | solution.py:89
  54.0 286.2 %all-reduce.5.cloned.1.call-start = ((), (), s32[]{:S(2)}) async-start(), calls=%async_computation.3 | async-start | bytes 1048576 | tf_op jit(solution)/shard_map/psum | solution.py:99
  54.3 6.2 copy-start.15
  60.6 93.3 %copy-start.16 = (pred[96]{0:T(512)(128)(4,1)}, pred[96]{0:T(512)(128)(4,1)S(1)}, u32[]{:S(2)}) copy-start(pred[96]{0:T(512)(128)(4,1)S(1)} %compare_and_fusion.1) | copy-start | bytes 292
  282.7 1.6 copy-start.18
  282.7 57.5 %copy-start.5 = (f32[8,128]{1,0:T(8,128)S(1)}, f32[8,128]{1,0:T(8,128)}, u32[]{:S(2)}) copy-start(f32[8,128]{1,0:T(8,128)} %param.14) | copy-start | bytes 12292
  282.7 57.5 %copy-start.8 = (f32[8,128]{1,0:T(8,128)S(1)}, f32[8,128]{1,0:T(8,128)}, u32[]{:S(2)}) copy-start(f32[8,128]{1,0:T(8,128)} %copy-done.7) | copy-start | bytes 12292
  282.7 57.5 %copy-start.11 = (f32[8,128]{1,0:T(8,128)S(1)}, f32[8,128]{1,0:T(8,128)}, u32[]{:S(2)}) copy-start(f32[8,128]{1,0:T(8,128)} %copy-done.10) | copy-start | bytes 12292
  282.7 57.5 %copy-start.20 = (f32[8,128]{1,0:T(8,128)S(1)}, f32[8,128]{1,0:T(8,128)}, u32[]{:S(2)}) copy-start(f32[8,128]{1,0:T(8,128)} %param.15) | copy-start | bytes 12292
  282.7 57.5 %copy-start.22 = (f32[8,128]{1,0:T(8,128)S(1)}, f32[8,128]{1,0:T(8,128)}, u32[]{:S(2)}) copy-start(f32[8,128]{1,0:T(8,128)} %param.13) | copy-start | bytes 12292
  284.3 57.3 %copy-start.1 = (f32[8,32,128]{2,0,1:T(8,128)S(1)}, f32[8,32,128]{2,0,1:T(8,128)}, u32[]{:S(2)}) copy-start(f32[8,32,128]{2,0,1:T(8,128)} %copy-done) | copy-start | bytes 393220
  286.0 452.8 %all-reduce.7.cloned.1.call-start = ((), (), s32[]{:S(2)}) async-start(), calls=%async_computation.4 | async-start | bytes 1048576 | tf_op jit(solution)/shard_map/psum | solution.py:99
  341.6 2.9 copy-start.3
  341.7 2.8 copy-start.14
  548.0 2.9 copy-start.17
  680.2 1.6 copy-start.19
  680.2 58.6 %copy-start.6 = (f32[8,128]{1,0:T(8,128)S(1)}, f32[8,128]{1,0:T(8,128)}, u32[]{:S(2)}) copy-start(f32[8,128]{1,0:T(8,128)} %param.14) | copy-start | bytes 12292
  680.2 58.6 %copy-start.9 = (f32[8,128]{1,0:T(8,128)S(1)}, f32[8,128]{1,0:T(8,128)}, u32[]{:S(2)}) copy-start(f32[8,128]{1,0:T(8,128)} %copy-done.7) | copy-start | bytes 12292
  680.2 58.6 %copy-start.12 = (f32[8,128]{1,0:T(8,128)S(1)}, f32[8,128]{1,0:T(8,128)}, u32[]{:S(2)}) copy-start(f32[8,128]{1,0:T(8,128)} %copy-done.10) | copy-start | bytes 12292
  680.2 58.6 %copy-start.21 = (f32[8,128]{1,0:T(8,128)S(1)}, f32[8,128]{1,0:T(8,128)}, u32[]{:S(2)}) copy-start(f32[8,128]{1,0:T(8,128)} %param.15) | copy-start | bytes 12292
  680.2 58.6 %copy-start.23 = (f32[8,128]{1,0:T(8,128)S(1)}, f32[8,128]{1,0:T(8,128)}, u32[]{:S(2)}) copy-start(f32[8,128]{1,0:T(8,128)} %param.13) | copy-start | bytes 12292
  681.8 58.4 %copy-start.2 = (f32[8,32,128]{2,0,1:T(8,128)S(1)}, f32[8,32,128]{2,0,1:T(8,128)}, u32[]{:S(2)}) copy-start(f32[8,32,128]{2,0,1:T(8,128)} %copy-done) | copy-start | bytes 393220
  681.8 58.4 %copy-start.4 = (f32[8,32,128]{2,0,1:T(8,128)S(1)}, f32[8,32,128]{2,0,1:T(8,128)}, u32[]{:S(2)}) copy-start(f32[8,32,128]{2,0,1:T(8,128)} %copy-done.3) | copy-start | bytes 393220
Sparse Core Ops, SparseCore 0:
  286.1 54.0 all-reduce.4
  683.7 55.1 all-reduce.6
where the time goes:
time: 761 us; the launch traced here: 748 us
  waiting for transfers between devices  211 us (28%)
  blocking collectives  201 us (26%)
  local copies, waits for them, and re-layouts  196 us (26%)
  matrix products  82.8 us (11%)
  starting transfers between devices  26.5 us (3%)
  other arithmetic  15.5 us (2%)
  between operations  14.7 us (2%)
    all_to_all x1, blocking collectives, local(): lax.all_to_all(outgoing, 'recv', split_axis=0, concat_axis=0, tiled=True)  201 us
    another operation x8, local copies, waits for them, and re-layouts, one_kernel(): jnp.stack(pieces, axis=2).reshape(per_kernel * BLOCK, lag_count * width)  130 us
    psum x2, waiting for transfers between devices, local(): summed_all = lax.psum(partial_terms, 'src')  109 us
    all_to_all x1, waiting for transfers between devices, local(): lax.all_to_all(outgoing, 'recv', split_axis=0, concat_axis=0, tiled=True)  89.8 us
    dot_general x8, matrix products, one_kernel(): jnp.einsum('mk,rk->mr', stacked_rows, kern, precision=lax.Precision.HIGHEST)  79.5 us
    all_to_all x1, starting transfers between devices, local(): lax.all_to_all(wanted.reshape(n_recv, peer_cap), 'recv', split_axis=0, co...  19.4 us
    gather x2, local copies, waits for them, and re-layouts, cut_window(): lax.dynamic_slice_in_dim(window, 2 * BLOCK - delay - (lag_count - 1), BLO...  17 us
    slice x8, local copies, waits for them, and re-layouts, one_kernel(): segs[:, lag_count - 1 - lag_idx:lag_count - 1 - lag_idx + BLOCK]  15.4 us
  transfers between devices with their start and end apart: 4, of which 4 were waited for; matrix products, arithmetic and copies ran while one was open for 1% of the time, Pallas kernels for 0%

commit v1 on v0

--- a/solution.py
+++ b/solution.py
@@ -96,7 +96,7 @@
             )
             summed = jnp.dot(route_table, stress_terms, precision=lax.Precision.HIGHEST)
             partial_terms = summed.reshape(group_rows, BLOCK, width)
-            summed_all = lax.psum(partial_terms, "src")
+            summed_all = jnp.sum(lax.all_gather(partial_terms, "src"), axis=0)
             stress = lax.dynamic_slice_in_dim(summed_all, src_idx * patch_count, patch_count, 0)
         times = (block_idx * BLOCK + 1 + jnp.arange(BLOCK, dtype=jnp.int32)).astype(jnp.float32)
         drive = prestress[:, None, :] + load_rate[:, None, :] * times[None, :, None] + stress

time: 761 us -> 725 us (0.953)
  the two profiles are of different devices: /device:TPU:2 before, /device:TPU:1 now
where the time goes in v1:
time: 725 us; the launch traced here: 712 us
  blocking collectives  201 us (28%)
  local copies, waits for them, and re-layouts  196 us (27%)
  waiting for transfers between devices  173 us (24%)
  matrix products  82.9 us (11%)
  starting transfers between devices  26.5 us (4%)
  other arithmetic  17.6 us (2%)
  between operations  14.5 us (2%)
    all_to_all x1, blocking collectives, local(): lax.all_to_all(outgoing, 'recv', split_axis=0, concat_axis=0, tiled=True)  201 us
    another operation x8, local copies, waits for them, and re-layouts, one_kernel(): jnp.stack(pieces, axis=2).reshape(per_kernel * BLOCK, lag_count * width)  131 us
    all_to_all x1, waiting for transfers between devices, local(): lax.all_to_all(outgoing, 'recv', split_axis=0, concat_axis=0, tiled=True)  90.9 us
    dot_general x8, matrix products, one_kernel(): jnp.einsum('mk,rk->mr', stacked_rows, kern, precision=lax.Precision.HIGHEST)  79.5 us
    all_gather x2, waiting for transfers between devices, local(): summed_all = jnp.sum(lax.all_gather(partial_terms, 'src'), axis=0)  69 us
    all_to_all x1, starting transfers between devices, local(): lax.all_to_all(wanted.reshape(n_recv, peer_cap), 'recv', split_axis=0, co...  20.4 us
    gather x2, local copies, waits for them, and re-layouts, cut_window(): lax.dynamic_slice_in_dim(window, 2 * BLOCK - delay - (lag_count - 1), BLO...  16.9 us
    slice x8, local copies, waits for them, and re-layouts, one_kernel(): segs[:, lag_count - 1 - lag_idx:lag_count - 1 - lag_idx + BLOCK]  15.3 us
  transfers between devices with their start and end apart: 4, of which 4 were waited for; matrix products, arithmetic and copies ran while one was open for 1% of the time, Pallas kernels for 0%

profile of v1, /device:TPU:1, one launch (start us, length us, event | category | flops | bytes accessed | tf_op | source)
XLA Modules:
  0.0 711.6 jit_solution(17583245619541114500)
XLA Ops:
  9.3 20.4 %all-to-all-start = ((s32[128,1,1]{2,1,0:T(1,128)}), s32[128,1,1]{2,1,0:T(1,128)S(1)}, u32[]{:S(2)}, u32[]{:S(2)}) async-start(s32[128,1,1]{2,1,0:T(1,128)} %copy.156), calls=%async_computation | async-start | bytes 131072 | tf_op jit(solution)/shard_map/all_to_all | solution.py:59
  31.5 13.0 %all-to-all-done = s32[128,1,1]{2,1,0:T(1,128)S(1)} async-done(((s32[128,1,1]{2,1,0:T(1,128)}), s32[128,1,1]{2,1,0:T(1,128)S(1)}, u32[]{:S(2)}, u32[]{:S(2)}) %all-to-all-start) | async-done | bytes 544 | tf_op jit(solution)/shard_map/all_to_all | solution.py:59
  44.5 2.3 reduce
  49.2 5.7 all-to-all-start.1
  55.3 4.9 reshape.363
  60.9 90.9 %all-to-all-done.1 = f32[128,1,32,128]{3,2,1,0:T(8,128)S(1)} async-done(((f32[128,1,32,128]{3,2,1,0:T(8,128)}), f32[128,1,32,128]{3,2,1,0:T(8,128)S(1)}, u32[]{:S(2)}, u32[]{:S(2)}) %all-to-all-start.1) | async-done | bytes 2097184 | tf_op jit(solution)/shard_map/all_to_all | solution.py:89
  156.6 8.5 %gather_fusion.4 = f32[96,47,128]{2,0,1:T(8,128)} fusion(f32[96,64,128]{2,0,1:T(8,128)S(1)} %pad.5.clone, s32[96]{0:T(128)S(1)} %get-tuple-element.145), kind=kCustom, calls=%fused_computation.4 | custom fusion | bytes 4621440 | tf_op jit(solution)/shard_map/vmap()/gather | solution.py:68
  166.4 118.3 %while.20 = (s32[]{:T(128)}, f32[4,768,128]{2,1,0:T(8,128)}, f32[4,24,47,128]{3,1,0,2:T(8,128)}, f32[4,128,2048]{2,1,0:T(8,128)}, s32[]{:T(128)}) while((s32[]{:T(128)}, f32[4,768,128]{2,1,0:T(8,128)}, f32[4,24,47,128]{3,1,0,2:T(8,128)}, f32[4,128,2048]{2,1,0:T(8,128)}, s32[]{:T(128)}) %tuple.92), condition=%wide.region_4.5_spmd, body=%wide.region_3.4_spmd.sunk | while | flops 2415919104 | bytes 35210304 | solution.py:94
  170.0 16.4 %stack.104 = f32[24,32,16,128]{3,2,1,0:T(8,128)} concatenate(f32[24,32,1,128]{3,2,1,0:T(1,128)} %bitcast.325, f32[24,32,1,128]{3,2,1,0:T(1,128)} %bitcast.324, f32[24,32,1,128]{3,2,1,0:T(1,128)} %bitcast.323, f32[24,32,1,128]{3,2,1,0:T(1,128)} %bitcast.322, f32[24,32,1,128]{3,2,1,0:T(1,128)} %bitcast.321, f32[24,32,1,128]{3,2,1,0:T(1,128)} %bitcast.320, ...), dimensions={2} | concatenate | bytes 12582912 | tf_op jit(solution)/shard_map/while/body/eval_jaxpr/stack | solution.py:78
  186.4 9.9 %fusion.111 = f32[4,768,128]{2,1,0:T(8,128)} fusion(f32[4,768,128]{2,1,0:T(8,128)} %get-tuple-element.267, s32[]{:T(128)} %get-tuple-element.266, f32[96,8,16,128]{3,2,1,0:T(8,128)} %bitcast.308, f32[4,128,2048]{2,1,0:T(8,128)} %get-tuple-element.274), kind=kOutput, calls=%fused_computation.10.clone.1 | convolution fusion | flops 2415919104 | bytes 7734272 | tf_op jit(solution)/shard_map/while/body/eval_jaxpr/mk,rk->mr/dot_general | solution.py:79
  199.5 16.4 %stack.104 = f32[24,32,16,128]{3,2,1,0:T(8,128)} concatenate(f32[24,32,1,128]{3,2,1,0:T(1,128)} %bitcast.325, f32[24,32,1,128]{3,2,1,0:T(1,128)} %bitcast.324, f32[24,32,1,128]{3,2,1,0:T(1,128)} %bitcast.323, f32[24,32,1,128]{3,2,1,0:T(1,128)} %bitcast.322, f32[24,32,1,128]{3,2,1,0:T(1,128)} %bitcast.321, f32[24,32,1,128]{3,2,1,0:T(1,128)} %bitcast.320, ...), dimensions={2} | concatenate | bytes 12582912 | tf_op jit(solution)/shard_map/while/body/eval_jaxpr/stack | solution.py:78
  215.8 10.0 %fusion.111 = f32[4,768,128]{2,1,0:T(8,128)} fusion(f32[4,768,128]{2,1,0:T(8,128)} %get-tuple-element.267, s32[]{:T(128)} %get-tuple-element.266, f32[96,8,16,128]{3,2,1,0:T(8,128)} %bitcast.308, f32[4,128,2048]{2,1,0:T(8,128)} %get-tuple-element.274), kind=kOutput, calls=%fused_computation.10.clone.1 | convolution fusion | flops 2415919104 | bytes 7734272 | tf_op jit(solution)/shard_map/while/body/eval_jaxpr/mk,rk->mr/dot_general | solution.py:79
  228.9 16.4 %stack.104 = f32[24,32,16,128]{3,2,1,0:T(8,128)} concatenate(f32[24,32,1,128]{3,2,1,0:T(1,128)} %bitcast.325, f32[24,32,1,128]{3,2,1,0:T(1,128)} %bitcast.324, f32[24,32,1,128]{3,2,1,0:T(1,128)} %bitcast.323, f32[24,32,1,128]{3,2,1,0:T(1,128)} %bitcast.322, f32[24,32,1,128]{3,2,1,0:T(1,128)} %bitcast.321, f32[24,32,1,128]{3,2,1,0:T(1,128)} %bitcast.320, ...), dimensions={2} | concatenate | bytes 12582912 | tf_op jit(solution)/shard_map/while/body/eval_jaxpr/stack | solution.py:78
  245.3 9.9 %fusion.111 = f32[4,768,128]{2,1,0:T(8,128)} fusion(f32[4,768,128]{2,1,0:T(8,128)} %get-tuple-element.267, s32[]{:T(128)} %get-tuple-element.266, f32[96,8,16,128]{3,2,1,0:T(8,128)} %bitcast.308, f32[4,128,2048]{2,1,0:T(8,128)} %get-tuple-element.274), kind=kOutput, calls=%fused_computation.10.clone.1 | convolution fusion | flops 2415919104 | bytes 7734272 | tf_op jit(solution)/shard_map/while/body/eval_jaxpr/mk,rk->mr/dot_general | solution.py:79
  258.4 16.4 %stack.104 = f32[24,32,16,128]{3,2,1,0:T(8,128)} concatenate(f32[24,32,1,128]{3,2,1,0:T(1,128)} %bitcast.325, f32[24,32,1,128]{3,2,1,0:T(1,128)} %bitcast.324, f32[24,32,1,128]{3,2,1,0:T(1,128)} %bitcast.323, f32[24,32,1,128]{3,2,1,0:T(1,128)} %bitcast.322, f32[24,32,1,128]{3,2,1,0:T(1,128)} %bitcast.321, f32[24,32,1,128]{3,2,1,0:T(1,128)} %bitcast.320, ...), dimensions={2} | concatenate | bytes 12582912 | tf_op jit(solution)/shard_map/while/body/eval_jaxpr/stack | solution.py:78
  274.8 9.9 %fusion.111 = f32[4,768,128]{2,1,0:T(8,128)} fusion(f32[4,768,128]{2,1,0:T(8,128)} %get-tuple-element.267, s32[]{:T(128)} %get-tuple-element.266, f32[96,8,16,128]{3,2,1,0:T(8,128)} %bitcast.308, f32[4,128,2048]{2,1,0:T(8,128)} %get-tuple-element.274), kind=kOutput, calls=%fused_computation.10.clone.1 | convolution fusion | flops 2415919104 | bytes 7734272 | tf_op jit(solution)/shard_map/while/body/eval_jaxpr/mk,rk->mr/dot_general | solution.py:79
  288.0 33.7 %all-gather.5.cloned.1.call-done = f32[128,32,128]{2,0,1:T(8,128)} async-done(((f32[32,32,128]{2,0,1:T(8,128)}), f32[128,32,128]{2,0,1:T(8,128)}) %all-gather.5.cloned.1.call-update) | async-done | bytes 2097168 | tf_op jit(solution)/shard_map/all_gather | solution.py:99
  324.1 2.8 gather_fusion.2
  326.9 2.5 fusion.24
  329.5 200.6 %all_to_all.25 = f32[128,1,64,128]{3,2,1,0:T(8,128)} all-to-all(f32[128,1,64,128]{3,2,1,0:T(8,128)S(1)} %fusion.24), channel_id=1, replica_groups=mesh['recv'=128,'src'=4] {'recv'}, dimensions={0} | all-to-all | bytes 8388608 | tf_op jit(solution)/shard_map/all_to_all | solution.py:89
  530.0 2.9 gather_fusion.3
  535.1 8.5 %gather_fusion.5 = f32[96,47,128]{2,0,1:T(8,128)} fusion(f32[96,64,128]{2,0,1:T(8,128)S(1)} %copy.163, s32[96]{0:T(128)S(1)} %get-tuple-element.145), kind=kCustom, calls=%fused_computation.5 | custom fusion | bytes 4621440 | tf_op jit(solution)/shard_map/vmap()/gather | solution.py:68
  544.8 118.0 %while.21 = (s32[]{:T(128)}, f32[4,768,128]{2,1,0:T(8,128)}, f32[4,24,47,128]{3,1,0,2:T(8,128)}, f32[4,128,2048]{2,1,0:T(8,128)}, s32[]{:T(128)}) while((s32[]{:T(128)}, f32[4,768,128]{2,1,0:T(8,128)}, f32[4,24,47,128]{3,1,0,2:T(8,128)}, f32[4,128,2048]{2,1,0:T(8,128)}, s32[]{:T(128)}) %tuple.91), condition=%wide.region_7.8_spmd, body=%wide.region_6.7_spmd.sunk | while | flops 2415919104 | bytes 35210304 | solution.py:94
  548.2 16.4 %stack.105 = f32[24,32,16,128]{3,2,1,0:T(8,128)} concatenate(f32[24,32,1,128]{3,2,1,0:T(1,128)} %bitcast.341, f32[24,32,1,128]{3,2,1,0:T(1,128)} %bitcast.340, f32[24,32,1,128]{3,2,1,0:T(1,128)} %bitcast.339, f32[24,32,1,128]{3,2,1,0:T(1,128)} %bitcast.338, f32[24,32,1,128]{3,2,1,0:T(1,128)} %bitcast.337, f32[24,32,1,128]{3,2,1,0:T(1,128)} %bitcast.336, ...), dimensions={2} | concatenate | bytes 12582912 | tf_op jit(solution)/shard_map/while/body/eval_jaxpr/stack | solution.py:78
  564.5 9.9 %fusion.115 = f32[4,768,128]{2,1,0:T(8,128)} fusion(f32[4,768,128]{2,1,0:T(8,128)} %get-tuple-element.282, s32[]{:T(128)} %get-tuple-element.281, f32[96,8,16,128]{3,2,1,0:T(8,128)} %bitcast.309, f32[4,128,2048]{2,1,0:T(8,128)} %get-tuple-element.289), kind=kOutput, calls=%fused_computation.20.clone.1 | convolution fusion | flops 2415919104 | bytes 7734272 | tf_op jit(solution)/shard_map/while/body/eval_jaxpr/mk,rk->mr/dot_general | solution.py:79
  577.6 16.4 %stack.105 = f32[24,32,16,128]{3,2,1,0:T(8,128)} concatenate(f32[24,32,1,128]{3,2,1,0:T(1,128)} %bitcast.341, f32[24,32,1,128]{3,2,1,0:T(1,128)} %bitcast.340, f32[24,32,1,128]{3,2,1,0:T(1,128)} %bitcast.339, f32[24,32,1,128]{3,2,1,0:T(1,128)} %bitcast.338, f32[24,32,1,128]{3,2,1,0:T(1,128)} %bitcast.337, f32[24,32,1,128]{3,2,1,0:T(1,128)} %bitcast.336, ...), dimensions={2} | concatenate | bytes 12582912 | tf_op jit(solution)/shard_map/while/body/eval_jaxpr/stack | solution.py:78
  594.0 10.0 %fusion.115 = f32[4,768,128]{2,1,0:T(8,128)} fusion(f32[4,768,128]{2,1,0:T(8,128)} %get-tuple-element.282, s32[]{:T(128)} %get-tuple-element.281, f32[96,8,16,128]{3,2,1,0:T(8,128)} %bitcast.309, f32[4,128,2048]{2,1,0:T(8,128)} %get-tuple-element.289), kind=kOutput, calls=%fused_computation.20.clone.1 | convolution fusion | flops 2415919104 | bytes 7734272 | tf_op jit(solution)/shard_map/while/body/eval_jaxpr/mk,rk->mr/dot_general | solution.py:79
  607.1 16.4 %stack.105 = f32[24,32,16,128]{3,2,1,0:T(8,128)} concatenate(f32[24,32,1,128]{3,2,1,0:T(1,128)} %bitcast.341, f32[24,32,1,128]{3,2,1,0:T(1,128)} %bitcast.340, f32[24,32,1,128]{3,2,1,0:T(1,128)} %bitcast.339, f32[24,32,1,128]{3,2,1,0:T(1,128)} %bitcast.338, f32[24,32,1,128]{3,2,1,0:T(1,128)} %bitcast.337, f32[24,32,1,128]{3,2,1,0:T(1,128)} %bitcast.336, ...), dimensions={2} | concatenate | bytes 12582912 | tf_op jit(solution)/shard_map/while/body/eval_jaxpr/stack | solution.py:78
  623.5 9.9 %fusion.115 = f32[4,768,128]{2,1,0:T(8,128)} fusion(f32[4,768,128]{2,1,0:T(8,128)} %get-tuple-element.282, s32[]{:T(128)} %get-tuple-element.281, f32[96,8,16,128]{3,2,1,0:T(8,128)} %bitcast.309, f32[4,128,2048]{2,1,0:T(8,128)} %get-tuple-element.289), kind=kOutput, calls=%fused_computation.20.clone.1 | convolution fusion | flops 2415919104 | bytes 7734272 | tf_op jit(solution)/shard_map/while/body/eval_jaxpr/mk,rk->mr/dot_general | solution.py:79
  636.5 16.4 %stack.105 = f32[24,32,16,128]{3,2,1,0:T(8,128)} concatenate(f32[24,32,1,128]{3,2,1,0:T(1,128)} %bitcast.341, f32[24,32,1,128]{3,2,1,0:T(1,128)} %bitcast.340, f32[24,32,1,128]{3,2,1,0:T(1,128)} %bitcast.339, f32[24,32,1,128]{3,2,1,0:T(1,128)} %bitcast.338, f32[24,32,1,128]{3,2,1,0:T(1,128)} %bitcast.337, f32[24,32,1,128]{3,2,1,0:T(1,128)} %bitcast.336, ...), dimensions={2} | concatenate | bytes 12582912 | tf_op jit(solution)/shard_map/while/body/eval_jaxpr/stack | solution.py:78
  652.9 9.9 %fusion.115 = f32[4,768,128]{2,1,0:T(8,128)} fusion(f32[4,768,128]{2,1,0:T(8,128)} %get-tuple-element.282, s32[]{:T(128)} %get-tuple-element.281, f32[96,8,16,128]{3,2,1,0:T(8,128)} %bitcast.309, f32[4,128,2048]{2,1,0:T(8,128)} %get-tuple-element.289), kind=kOutput, calls=%fused_computation.20.clone.1 | convolution fusion | flops 2415919104 | bytes 7734272 | tf_op jit(solution)/shard_map/while/body/eval_jaxpr/mk,rk->mr/dot_general | solution.py:79
  666.1 35.3 %all-gather.7.cloned.1.call-done = f32[128,32,128]{2,0,1:T(8,128)} async-done(((f32[32,32,128]{2,0,1:T(8,128)}), f32[128,32,128]{2,0,1:T(8,128)}) %all-gather.7.cloned.1.call-update) | async-done | bytes 2097168 | tf_op jit(solution)/shard_map/all_gather | solution.py:99
  (78 shorter events, 53.9 us)
Async XLA Ops:
  9.3 35.2 %all-to-all-start = ((s32[128,1,1]{2,1,0:T(1,128)}), s32[128,1,1]{2,1,0:T(1,128)S(1)}, u32[]{:S(2)}, u32[]{:S(2)}) async-start(s32[128,1,1]{2,1,0:T(1,128)} %copy.156), calls=%async_computation | async-start | bytes 131072 | tf_op jit(solution)/shard_map/all_to_all | solution.py:59
  49.2 102.6 %all-to-all-start.1 = ((f32[128,1,32,128]{3,2,1,0:T(8,128)}), f32[128,1,32,128]{3,2,1,0:T(8,128)S(1)}, u32[]{:S(2)}, u32[]{:S(2)}) async-start(f32[128,1,32,128]{3,2,1,0:T(8,128)} %fusion.25), calls=%async_computation.1 | async-start | bytes 4194304 | tf_op jit(solution)/shard_map/all_to_all | solution.py:89
  54.9 266.8 %all-gather.5.cloned.1.call-start = ((), (), s32[]{:S(2)}) async-start(), calls=%async_computation.3 | async-start | bytes 2621440 | tf_op jit(solution)/shard_map/all_gather | solution.py:99
  55.3 5.6 copy-start.1
  287.9 35.7 %copy-start = (f32[8,128]{1,0:T(8,128)S(1)}, f32[8,128]{1,0:T(8,128)}, u32[]{:S(2)}) copy-start(f32[8,128]{1,0:T(8,128)} %param.14) | copy-start | bytes 12292
  287.9 35.7 %copy-start.2 = (f32[8,128]{1,0:T(8,128)S(1)}, f32[8,128]{1,0:T(8,128)}, u32[]{:S(2)}) copy-start(f32[8,128]{1,0:T(8,128)} %param.15) | copy-start | bytes 12292
  287.9 35.7 %copy-start.3 = (f32[8,128]{1,0:T(8,128)S(1)}, f32[8,128]{1,0:T(8,128)}, u32[]{:S(2)}) copy-start(f32[8,128]{1,0:T(8,128)} %param.13) | copy-start | bytes 12292
  287.9 413.4 %all-gather.7.cloned.1.call-start = ((), (), s32[]{:S(2)}) async-start(), calls=%async_computation.4 | async-start | bytes 2621440 | tf_op jit(solution)/shard_map/all_gather | solution.py:99
Sparse Core Ops, SparseCore 0:
  288.1 33.6 all-gather.4
  666.2 35.1 all-gather.6
